TPU v7x, 32 devices: a whole 2x2x4 slice. The times are simulated.
32 devices in a mesh: parts: 2 (over y), blk: 8 (over z, x), gshard: 2 (over core).
Axes of the slice: x: 2, y: 2, z: 4, core: 2. Of those that a mesh axis runs over, the one named last changes fastest.
Arguments:
- screened: bfloat16 [4, 16384, 16384], P('parts', ('blk', 'gshard')), parts along dimension 0, may hold values from -0.046875 to 0.046875
- pairs: bfloat16 [64, 16, 16384], P('parts', None, ('blk', 'gshard')), parts along dimension 0, may hold values from -0.625 to 0.625
- energies: float32 [32], P('parts'), parts along dimension 0, may hold values from -1.5 to 1.5
- nodes: float32 [4], P('parts'), parts along dimension 0, may hold values from 0.2 to 2
- qweights: float32 [4], P('parts'), parts along dimension 0, may hold values from 0.5 to 2
Outputs:
- sigma: float32 [4, 1024], P('parts', ('blk', 'gshard')), parts along dimension 0
There are 2 independent parts, one for each index of `parts`. A program takes and returns all parts, laid end to end along the dimension named above; each array names one. Nothing has to cross between parts.
All inputs are finite; a program needn't handle non-finite values.
Results may differ from a plain program's by a relative error of at most 0.0029.
Values may be sent and summed in bfloat16 or wider, within the bound.
A program may use at most 192 MiB of HBM per device.

v0:
```python
import jax
import jax.numpy as jnp
from jax import lax
from jax.sharding import PartitionSpec as P


def local(screened, pairs, energies, nodes, qweights):
    nodes_count, rows_here, plane_total = screened.shape
    targets, summed, _ = pairs.shape
    pair_rows = targets * summed
    weights_flat = screened.reshape(nodes_count * rows_here, plane_total)
    piece = lax.all_gather(pairs, ("blk", "gshard"), axis=2, tiled=True)
    width = piece.shape[2]
    product = lax.dot_general(
        weights_flat,
        piece.reshape(pair_rows, width),
        (((1,), (1,)), ((), ())),
        preferred_element_type=jnp.float32,
    )
    coupling = (
        qweights[:, None] * energies[None, :] / (energies[None, :] ** 2 + nodes[:, None] ** 2)
    )
    scaled = (
        product.reshape(nodes_count, rows_here, targets, summed) * coupling[:, None, None, :]
    ).astype(jnp.bfloat16)
    partial_sigma = jnp.einsum(
        "nkg,fgmk->fnm", pairs, scaled, preferred_element_type=jnp.float32
    ).reshape(nodes_count, targets * targets)
    grouped = lax.psum_scatter(partial_sigma, "blk", scatter_dimension=1, tiled=True)
    sigma = lax.psum_scatter(grouped, "gshard", scatter_dimension=1, tiled=True)
    return sigma


def solution(mesh):
    placed = (
        P("parts", ("blk", "gshard"), None),
        P("parts", None, ("blk", "gshard")),
        P("parts"),
        P("parts"),
        P("parts"),
    )
    return jax.shard_map(
        local, mesh=mesh, in_specs=placed, out_specs=P("parts", ("blk", "gshard")), check_vma=False
    )
```

profile of v0, /device:TPU:0, one launch (start us, length us, event | category | flops | bytes accessed | tf_op | source)
XLA Modules:
  0.0 261.6 jit_solution(12047633297926874790)
XLA Ops:
  6.5 0.0 all-gather.2.cloned.1.call-start
  6.5 2.8 %copy.9 = bf16[32,16,1024]{2,0,1:T(8,128)(2,1)} copy(bf16[32,16,1024]{2,1,0:T(8,128)(2,1)} %param.6) | data formatting | bytes 2097152 | tf_op args[1]
  9.3 0.0 all-gather.2.cloned.1.call-update
  9.3 0.0 reduce-scatter.7.cloned.1.call-start
  9.4 0.7 integer_pow.9
  10.1 0.7 integer_pow.8
  10.9 0.7 add_divide_fusion
  11.6 0.0 copy-start
  11.6 127.6 %all-gather.2.cloned.1.call-done = bf16[32,16,16384]{2,0,1:T(8,128)(2,1)} async-done(((bf16[32,16,1024]{2,0,1:T(8,128)(2,1)}), bf16[32,16,16384]{2,0,1:T(8,128)(2,1)}) %all-gather.2.cloned.1.call-update) | async-done | bytes 16777232 | tf_op jit(solution)/shard_map/all_gather | solution.py:12
  139.2 42.6 %multiply_convert_fusion = bf16[2,1024,32,16]{1,2,3,0:T(8,128)(2,1)S(1)} fusion(bf16[32,16,16384]{2,0,1:T(8,128)(2,1)} %all-gather.2.cloned.1.call-done, bf16[2,1024,16384]{2,1,0:T(8,128)(2,1)} %param.5, f32[2,16]{1,0:T(2,128)S(1)} %add_divide_fusion), kind=kOutput, calls=%fused_computation.3 | convolution fusion | flops 34361835520 | bytes 85983360 | tf_op jit(solution)/shard_map/dot_general | solution.py:14
  181.8 0.0 copy-done
  181.8 1.5 convolution_bitcast_fusion
  183.3 1.3 copy.18
  184.6 0.0 reduce-scatter.7.cloned.1.call-update
  184.6 0.0 reduce-scatter.9.cloned.1.call-start
  184.7 60.3 %reduce-scatter.7.cloned.1.call-done = f32[128,2]{1,0:T(8,128)} async-done(((f32[1024,2]{1,0:T(8,128)}), f32[128,2]{1,0:T(8,128)}) %reduce-scatter.7.cloned.1.call-update) | async-done | bytes 1040
  244.9 0.0 reduce-scatter.9.cloned.1.call-update
  244.9 8.7 %reduce-scatter.9.cloned.1.call-done = f32[64,2]{1,0:T(8,128)} async-done(((f32[128,2]{1,0:T(8,128)}), f32[64,2]{1,0:T(8,128)}) %reduce-scatter.9.cloned.1.call-update) | async-done | bytes 528
  253.7 1.4 copy.17
Async XLA Ops:
  6.5 132.6 %all-gather.2.cloned.1.call-start = ((), (), s32[]{:S(2)}) async-start(), calls=%async_computation.2 | async-start | bytes 17825792 | tf_op jit(solution)/shard_map/all_gather | solution.py:12
  9.3 235.6 %reduce-scatter.7.cloned.1.call-start = ((), (), s32[]{:S(2)}) async-start(), calls=%async_computation.3 | async-start | bytes 589824
  11.6 170.2 %copy-start = (bf16[32,16,1024]{2,1,0:T(8,128)(2,1)S(1)}, bf16[32,16,1024]{2,1,0:T(8,128)(2,1)}, u32[]{:S(2)}) copy-start(bf16[32,16,1024]{2,1,0:T(8,128)(2,1)} %param.6) | copy-start | bytes 3145732
  184.6 69.1 %reduce-scatter.9.cloned.1.call-start = ((), (), s32[]{:S(2)}) async-start(), calls=%async_computation.4 | async-start | bytes 98304
Sparse Core Ops, SparseCore 0:
  9.5 129.5 all-gather.1
  184.7 60.1 reduce-scatter.6
  247.2 6.4 reduce-scatter.8
where the time goes:
time: 262 us
  waiting for transfers between devices  197 us (75%)
  matrix products  44.1 us (17%)
  between operations  13.1 us (5%)
  local copies, waits for them, and re-layouts  5.44 us (2%)
    all_gather x1, waiting for transfers between devices, local(): piece = lax.all_gather(pairs, ('blk', 'gshard'), axis=2, tiled=True)  128 us
    unnamed x5, waiting for transfers between devices  69 us
    dot_general x1, matrix products, local(): lax.dot_general(weights_flat, piece.reshape(pair_rows, width), (((1,), (1...  42.6 us
    unnamed x5, local copies, waits for them, and re-layouts  5.44 us
  transfers between devices with their start and end apart: 3, of which 3 were waited for; matrix products, arithmetic and copies ran while one was open for 1% of the time, Pallas kernels for 0%

commit v1 on v0

v1 whole, which is shorter than its diff:
```python
import functools

import jax
import jax.numpy as jnp
from jax import lax
from jax.experimental import pallas as pl
from jax.experimental.pallas import tpu as pltpu
from jax.sharding import PartitionSpec as P

MESH = pl.DeviceIdType.MESH
SLOTS = 3


def grid_of(chips):
    across = 1
    while chips % (2 * across) == 0 and 2 * (2 * across) ** 2 <= chips:
        across *= 2
    return chips // across, across


def place_of(chip, deep, across):
    z, x = lax.div(chip, across), lax.rem(chip, across)
    row = deep - 1 - z
    column = jnp.where(lax.rem(row, 2) == 0, x - 1, across - 1 - x)
    return jnp.where(x == 0, z, deep + row * (across - 1) + column)


def chip_of(place, deep, across):
    if across == 1:
        return place
    past = jnp.maximum(place - deep, 0)
    row, column = lax.div(past, across - 1), lax.rem(past, across - 1)
    x = jnp.where(lax.rem(row, 2) == 0, 1 + column, across - 1 - column)
    return jnp.where(place < deep, place * across, (deep - 1 - row) * across + x)


def kernel(chips, targets, summed, w_hbm, own, energies, nodes, qweights, out, buf, sib_own, w_buf, acc, coup, red_send,
           red_recv, w_sem, send_sem, recv_sem, pass_sem, sib_sem, red_ssem, red_rsem):
    count, rows = w_buf.shape[1], w_buf.shape[2]
    half = buf.shape[2]
    steps = buf.shape[1]
    devices = 2 * chips
    share = red_recv.shape[1]
    group = max(1, devices // targets)
    deep, across = grid_of(chips)
    blk, core = lax.axis_index("blk"), lax.axis_index("gshard")
    me = blk * 2 + core
    other = 1 - core
    place = place_of(blk, deep, across)
    right = chip_of(lax.rem(place + 1, chips), deep, across)
    left = chip_of(lax.rem(place + chips - 1, chips), deep, across)

    def column_block(s):
        u = jnp.maximum(s - 2, 0)
        t, i = lax.div(u, 4), lax.rem(u, 4)
        distance = lax.div(t, 2) + 1
        spot = jnp.where(lax.rem(i, 2) == 0, place + chips - distance, place + distance)
        chip = chip_of(lax.rem(spot, chips), deep, across)
        holder = jnp.where(i < 2, core, other)
        block = chip * 2 + holder
        return jnp.where(s == 0, me, jnp.where(s == 1, blk * 2 + other, block))

    def w_copy(s):
        slot = lax.rem(s, SLOTS)
        start = pl.multiple_of(column_block(s) * rows, rows)
        return pltpu.make_async_copy(w_hbm.at[:, :, pl.ds(start, rows)], w_buf.at[slot], w_sem.at[slot])

    total = 2 + 4 * steps
    for s in range(SLOTS - 1):
        w_copy(jnp.int32(s)).start()

    barrier = pltpu.get_barrier_semaphore()

    def device(j):
        return {"blk": lax.div(j, 2), "gshard": lax.rem(j, 2)}

    def greet(o, carry):
        pl.semaphore_signal(barrier, inc=1, device_id=device(lax.rem(me + o, devices)), device_id_type=MESH)
        return carry

    lax.fori_loop(1, devices, greet, 0)
    pl.semaphore_wait(barrier, devices - 1)

    def ring_copy(src, way, t):
        return pltpu.make_async_remote_copy(
            src_ref=src, dst_ref=buf.at[way, t], send_sem=send_sem.at[way, t], recv_sem=recv_sem.at[way, t],
            device_id={"blk": right if way == 0 else left, "gshard": core}, device_id_type=MESH)

    def pass_copy(way, t):
        return pltpu.make_async_remote_copy(
            src_ref=buf.at[way, t], dst_ref=buf.at[2 + way, t], send_sem=pass_sem.at[way, t],
            recv_sem=recv_sem.at[2 + way, t], device_id={"blk": blk, "gshard": other}, device_id_type=MESH)

    for t in range(min(2, steps)):
        for way in range(2):
            h = t if way == 0 else 1 - t
            ring_copy(own.at[pl.ds(h * half, half)], way, t).start()
    sib_copy = pltpu.make_async_remote_copy(
        src_ref=own, dst_ref=sib_own, send_sem=sib_sem.at[0], recv_sem=sib_sem.at[1],
        device_id={"blk": blk, "gshard": other}, device_id_type=MESH)
    sib_copy.start()

    lane = lax.broadcasted_iota(jnp.int32, (1, half), 1)
    lane_k = lax.rem(lane, summed)
    e_row = jnp.zeros((1, half), jnp.float32)
    for k in range(summed):
        e_row = jnp.where(lane_k == k, energies[k], e_row)
    for f in range(count):
        coup[f] = qweights[f] * e_row / (e_row * e_row + nodes[f] * nodes[f])

    def product(slot, f, piece):
        return lax.dot_general(w_buf[slot, f], piece, (((1,), (1,)), ((), ())), preferred_element_type=jnp.float32)

    def next_w(s):
        @pl.when(s + SLOTS - 1 < total)
        def _():
            w_copy(s + SLOTS - 1).start()

    next_w(jnp.int32(0))
    w_copy(jnp.int32(0)).wait()

    def first(v, carry):
        h, f = lax.div(v, count), lax.rem(v, count)
        acc[h, f] = product(0, f, own[pl.ds(pl.multiple_of(h * half, half), half), :])
        return carry

    lax.fori_loop(0, 2 * count, first, 0)
    next_w(jnp.int32(1))
    w_copy(jnp.int32(1)).wait()
    sib_copy.wait_recv()

    def second(v, carry):
        h, f = lax.div(v, count), lax.rem(v, count)
        acc[h, f] += product(1 % SLOTS, f, sib_own[pl.ds(pl.multiple_of(h * half, half), half), :])
        return carry

    lax.fori_loop(0, 2 * count, second, 0)

    def step(t, carry):
        for way in range(2):
            ring_copy(buf.at[way, t], way, t).wait_recv()

            @pl.when(t + 2 < steps)
            def _():
                ring_copy(buf.at[way, t], way, t + 2).start()

            pass_copy(way, t).start()

        def unit(i, carry):
            s = 2 + 4 * t + i
            next_w(s)
            for way in range(2):
                @pl.when(i == 2 + way)
                def _():
                    pass_copy(way, t).wait_recv()
            w_copy(s).wait()
            slot = lax.rem(s, SLOTS)
            h = lax.rem(t + i, 2)

            def node(f, carry):
                acc[h, f] += product(slot, f, buf[i, t])
                return carry

            lax.fori_loop(0, count, node, 0)
            return carry

        lax.fori_loop(0, 4, unit, 0)
        return carry

    lax.fori_loop(0, steps, step, 0)

    pair_rows = own.shape[0]
    row_k = lax.rem(lax.broadcasted_iota(jnp.int32, (pair_rows, half), 0), summed)
    same = row_k == lax.rem(lax.broadcasted_iota(jnp.int32, (pair_rows, half), 1), summed)
    for f in range(count):
        for h in range(2):
            scaled = (acc[h, f] * coup[f]).astype(jnp.bfloat16)
            part = jnp.dot(own[...], scaled, preferred_element_type=jnp.float32)
            kept = jnp.where(same, part, 0.0).reshape(targets, summed, half).sum(axis=1)
            for n in range(targets):
                red_send[n, pl.ds(f, 1), pl.ds(h * half, half)] = kept[n:n + 1, :]

    def red_copy(j):
        return pltpu.make_async_remote_copy(
            src_ref=red_send.at[pl.ds(lax.div(j, group) * share, share)], dst_ref=red_recv.at[me],
            send_sem=red_ssem.at[j], recv_sem=red_rsem.at[me], device_id=device(j), device_id_type=MESH)

    def send(o, carry):
        red_copy(lax.rem(me + o, devices)).start()
        return carry

    lax.fori_loop(1, devices, send, 0)

    def arrive(o, so_far):
        j = lax.rem(me + o, devices)
        pltpu.make_async_remote_copy(
            src_ref=red_send.at[pl.ds(0, share)], dst_ref=red_recv.at[j], send_sem=red_ssem.at[j],
            recv_sem=red_rsem.at[j], device_id=device(j), device_id_type=MESH).wait_recv()
        return so_far + red_recv[j]

    out[...] = lax.fori_loop(1, devices, arrive, red_send[pl.ds(lax.div(me, group) * share, share)])

    def sent(o, carry):
        red_copy(lax.rem(me + o, devices)).wait_send()
        return carry

    lax.fori_loop(1, devices, sent, 0)
    sib_copy.wait_send()

    def drained(t, carry):
        for way in range(2):
            ring_copy(buf.at[way, 0], way, t).wait_send()
            pass_copy(way, t).wait_send()
        return carry

    lax.fori_loop(0, steps, drained, 0)


def local(chips, screened, pairs, energies, nodes, qweights):
    count, rows, plane_total = screened.shape
    targets, summed, _ = pairs.shape
    pair_rows = targets * summed
    half = pair_rows // 2
    steps = chips - 1
    devices = 2 * chips
    share = max(1, targets // devices)
    smem = pl.BlockSpec(memory_space=pltpu.SMEM)
    vmem = pl.BlockSpec(memory_space=pltpu.VMEM)
    dma = pltpu.SemaphoreType.DMA
    grouped = pl.pallas_call(
        functools.partial(kernel, chips, targets, summed),
        out_shape=jax.ShapeDtypeStruct((share, count, pair_rows), jnp.float32),
        in_specs=[pl.BlockSpec(memory_space=pl.ANY), vmem, smem, smem, smem],
        out_specs=vmem,
        scratch_shapes=[
            pltpu.VMEM((4, steps, half, rows), jnp.bfloat16),
            pltpu.VMEM((pair_rows, rows), jnp.bfloat16),
            pltpu.VMEM((SLOTS, count, rows, rows), jnp.bfloat16),
            pltpu.VMEM((2, count, rows, half), jnp.float32),
            pltpu.VMEM((count, 1, half), jnp.float32),
            pltpu.VMEM((targets, count, pair_rows), jnp.float32),
            pltpu.VMEM((devices, share, count, pair_rows), jnp.float32),
            dma((SLOTS,)),
            dma((2, steps)),
            dma((4, steps)),
            dma((2, steps)),
            dma((2,)),
            dma((devices,)),
            dma((devices,)),
        ],
        compiler_params=pltpu.CompilerParams(
            collective_id=0, has_side_effects=True, vmem_limit_bytes=56 * 1024 * 1024
        ),
        cost_estimate=pl.CostEstimate(
            flops=2 * count * rows * plane_total * pair_rows,
            bytes_accessed=4 * count * rows * plane_total,
            transcendentals=0,
        ),
    )(screened, pairs.reshape(pair_rows, rows), energies, nodes, qweights)
    sigma = grouped.reshape(share, count, targets, summed).sum(axis=3)
    sigma = sigma.transpose(1, 0, 2).reshape(count, share * targets)
    width = targets * targets // devices
    if width < share * targets:
        me = lax.axis_index("blk") * 2 + lax.axis_index("gshard")
        start = lax.rem(me, (share * targets) // width) * width
        sigma = lax.dynamic_slice_in_dim(sigma, start, width, axis=1)
    return sigma


def solution(mesh):
    placed = (
        P("parts", ("blk", "gshard"), None),
        P("parts", None, ("blk", "gshard")),
        P("parts"),
        P("parts"),
        P("parts"),
    )
    return jax.shard_map(
        functools.partial(local, mesh.shape["blk"]),
        mesh=mesh, in_specs=placed, out_specs=P("parts", ("blk", "gshard")), check_vma=False,
    )
```

time: 262 us -> 103 us (0.39)
  waiting for transfers between devices: 197 us -> 0 us
  Pallas kernels: 0 us -> 101 us
  matrix products: 44.1 us -> 0 us
  between operations: 13.1 us -> 0.03 us
  local copies, waits for them, and re-layouts: 5.44 us -> 1.43 us
    all_gather x1 -> x0, waiting for transfers between devices: 128 us -> none  [local(): piece = lax.all_gather(pairs, ('blk', 'gshard'), axis=2, tiled=True)]
    pallas_call x0 -> x1, Pallas kernels: none -> 101 us  [local(): pl.pallas_call(functools.partial(kernel, chips, targets, summed), out_sha...]
    unnamed x5 -> x0, waiting for transfers between devices: 69 us -> none
    dot_general x2 -> x0, matrix products: 44.1 us -> none  [the longest x1 42.6 us: local(): lax.dot_general(weights_flat, piece.reshape(pair_rows, width), (((1,), (1...]
    unnamed x5 -> x0, local copies, waits for them, and re-layouts: 5.44 us -> none
  transfers between devices with their start and end apart: 3 -> 0, of which waited for: 3 -> 0; matrix products, arithmetic and copies ran while one was open for 1% -> 0% of each run, Pallas kernels for 0% -> 0%
where the time goes in v1:
time: 103 us; the launch traced here: 102 us
  Pallas kernels  101 us (98%)
  local copies, waits for them, and re-layouts  1.43 us (1%)
    pallas_call x1, Pallas kernels, local(): pl.pallas_call(functools.partial(kernel, chips, targets, summed), out_sha...  101 us

profile of v1, /device:TPU:0, one launch (start us, length us, event | category | flops | bytes accessed | tf_op | source)
XLA Modules:
  0.0 102.4 jit_solution(18129134570783342222)
XLA Ops:
  0.0 100.9 %shard_map.55 = f32[2,2,512]{2,1,0:T(2,128)} custom-call(bf16[2,1024,16384]{2,1,0:T(8,128)(2,1)} %w_hbm.1, bf16[512,1024]{1,0:T(8,128)(2,1)} %bitcast.3, f32[16]{0:T(128)} %energies.1, f32[2]{0:T(128)} %nodes.1, f32[2]{0:T(128)} %qweights.1), custom_call_target="tpu_custom_call" | custom-call | flops 34359738368 | bytes 134217728 | tf_op jit(solution)/shard_map/pallas_call | solution.py:230
  100.9 0.8 reshape.10
  101.7 0.1 reduce_sum.9
  101.8 0.6 reshape.11
  (1 shorter events, 0.0 us)

commit v2 on v1

--- a/solution.py
+++ b/solution.py
@@ -34,7 +34,7 @@
     return jnp.where(place < deep, place * across, (deep - 1 - row) * across + x)
 
 
-def kernel(chips, targets, summed, w_hbm, own, energies, nodes, qweights, out, buf, sib_own, w_buf, acc, coup, red_send,
+def kernel(chips, targets, summed, w_hbm, own, energies, nodes, qweights, out, buf, sib_own, w_buf, acc, far, parts, coup, red_send,
            red_recv, w_sem, send_sem, recv_sem, pass_sem, sib_sem, red_ssem, red_rsem):
     count, rows = w_buf.shape[1], w_buf.shape[2]
     half = buf.shape[2]
@@ -51,7 +51,7 @@
     left = chip_of(lax.rem(place + chips - 1, chips), deep, across)
 
     def column_block(s):
-        u = jnp.maximum(s - 2, 0)
+        u = jnp.where(s < 4, 4 * (steps - 1) + 2 * jnp.maximum(s - 2, 0), s - 4)
         t, i = lax.div(u, 4), lax.rem(u, 4)
         distance = lax.div(t, 2) + 1
         spot = jnp.where(lax.rem(i, 2) == 0, place + chips - distance, place + distance)
@@ -65,7 +65,8 @@
         start = pl.multiple_of(column_block(s) * rows, rows)
         return pltpu.make_async_copy(w_hbm.at[:, :, pl.ds(start, rows)], w_buf.at[slot], w_sem.at[slot])
 
-    total = 2 + 4 * steps
+    total = 4 + 4 * (steps - 1)
+    last = steps - 1
     for s in range(SLOTS - 1):
         w_copy(jnp.int32(s)).start()
 
@@ -136,6 +137,21 @@
 
     lax.fori_loop(0, 2 * count, second, 0)
 
+    def from_rows(side, carry):
+        s = 2 + side
+        next_w(s)
+        w_copy(s).wait()
+        slot = lax.rem(s, SLOTS)
+
+        def node(f, carry):
+            far[side, f] = jnp.dot(own[...], w_buf[slot, f], preferred_element_type=jnp.float32).astype(jnp.bfloat16)
+            return carry
+
+        lax.fori_loop(0, count, node, 0)
+        return carry
+
+    lax.fori_loop(0, 2, from_rows, 0)
+
     def step(t, carry):
         for way in range(2):
             ring_copy(buf.at[way, t], way, t).wait_recv()
@@ -147,7 +163,7 @@
             pass_copy(way, t).start()
 
         def unit(i, carry):
-            s = 2 + 4 * t + i
+            s = 4 + 4 * t + i
             next_w(s)
             for way in range(2):
                 @pl.when(i == 2 + way)
@@ -167,15 +183,31 @@
         lax.fori_loop(0, 4, unit, 0)
         return carry
 
-    lax.fori_loop(0, steps, step, 0)
+    lax.fori_loop(0, last, step, 0)
+
+    for f in range(count):
+        for h in range(2):
+            scaled = (acc[h, f] * coup[f]).astype(jnp.bfloat16)
+            parts[h, f] = jnp.dot(own[...], scaled, preferred_element_type=jnp.float32)
+
+    def met(side, f, h):
+        return coup[f] * lax.dot_general(
+            far[side, f], buf[2 * side + h, last], (((1,), (1,)), ((), ())), preferred_element_type=jnp.float32)
+
+    for way in range(2):
+        ring_copy(buf.at[way, last], way, last).wait_recv()
+        pass_copy(way, last).start()
+    for h in range(2):
+        for f in range(count):
+            parts[h, f] += met(0, f, h)
 
     pair_rows = own.shape[0]
     row_k = lax.rem(lax.broadcasted_iota(jnp.int32, (pair_rows, half), 0), summed)
     same = row_k == lax.rem(lax.broadcasted_iota(jnp.int32, (pair_rows, half), 1), summed)
-    for f in range(count):
-        for h in range(2):
-            scaled = (acc[h, f] * coup[f]).astype(jnp.bfloat16)
-            part = jnp.dot(own[...], scaled, preferred_element_type=jnp.float32)
+    for h in range(2):
+        pass_copy(h, last).wait_recv()
+        for f in range(count):
+            part = parts[h, f] + met(1, f, h)
             kept = jnp.where(same, part, 0.0).reshape(targets, summed, half).sum(axis=1)
             for n in range(targets):
                 red_send[n, pl.ds(f, 1), pl.ds(h * half, half)] = kept[n:n + 1, :]
@@ -237,6 +269,8 @@
             pltpu.VMEM((pair_rows, rows), jnp.bfloat16),
             pltpu.VMEM((SLOTS, count, rows, rows), jnp.bfloat16),
             pltpu.VMEM((2, count, rows, half), jnp.float32),
+            pltpu.VMEM((2, count, pair_rows, rows), jnp.bfloat16),
+            pltpu.VMEM((2, count, pair_rows, half), jnp.float32),
             pltpu.VMEM((count, 1, half), jnp.float32),
             pltpu.VMEM((targets, count, pair_rows), jnp.float32),
             pltpu.VMEM((devices, share, count, pair_rows), jnp.float32),

time: 103 us -> 98.9 us (0.960)
  Pallas kernels: 101 us -> 97.1 us
    pallas_call x1, Pallas kernels: 101 us -> 97.1 us  [local(): pl.pallas_call(functools.partial(kernel, chips, targets, summed), out_sha...]
where the time goes in v2:
time: 98.9 us; the launch traced here: 98.7 us
  Pallas kernels  97.1 us (98%)
  local copies, waits for them, and re-layouts  1.43 us (1%)
    pallas_call x1, Pallas kernels, local(): pl.pallas_call(functools.partial(kernel, chips, targets, summed), out_sha...  97.1 us

profile of v2, /device:TPU:0, one launch (start us, length us, event | category | flops | bytes accessed | tf_op | source)
XLA Modules:
  0.0 98.7 jit_solution(3789911804126310717)
XLA Ops:
  0.0 97.1 %shard_map.55 = f32[2,2,512]{2,1,0:T(2,128)} custom-call(bf16[2,1024,16384]{2,1,0:T(8,128)(2,1)} %w_hbm.1, bf16[512,1024]{1,0:T(8,128)(2,1)} %bitcast.3, f32[16]{0:T(128)} %energies.1, f32[2]{0:T(128)} %nodes.1, f32[2]{0:T(128)} %qweights.1), custom_call_target="tpu_custom_call" | custom-call | flops 34359738368 | bytes 134217728 | tf_op jit(solution)/shard_map/pallas_call | solution.py:262
  97.1 0.8 reshape.10
  97.9 0.1 reduce_sum.9
  98.0 0.6 reshape.11
  (1 shorter events, 0.0 us)

commit v3 on v2

--- a/solution.py
+++ b/solution.py
@@ -35,7 +35,7 @@
 
 
 def kernel(chips, targets, summed, w_hbm, own, energies, nodes, qweights, out, buf, sib_own, w_buf, acc, far, parts, coup, red_send,
-           red_recv, w_sem, send_sem, recv_sem, pass_sem, sib_sem, red_ssem, red_rsem):
+           red_recv, w_sem, cut_send, cut_recv, cut_pass, send_sem, recv_sem, pass_sem, sib_sem, red_ssem, red_rsem):
     count, rows = w_buf.shape[1], w_buf.shape[2]
     half = buf.shape[2]
     steps = buf.shape[1]
@@ -75,12 +75,9 @@
     def device(j):
         return {"blk": lax.div(j, 2), "gshard": lax.rem(j, 2)}
 
-    def greet(o, carry):
-        pl.semaphore_signal(barrier, inc=1, device_id=device(lax.rem(me + o, devices)), device_id_type=MESH)
-        return carry
-
-    lax.fori_loop(1, devices, greet, 0)
-    pl.semaphore_wait(barrier, devices - 1)
+    for chip, holder in ((left, core), (right, core), (blk, other)):
+        pl.semaphore_signal(barrier, inc=1, device_id={"blk": chip, "gshard": holder}, device_id_type=MESH)
+    pl.semaphore_wait(barrier, 3)
 
     def ring_copy(src, way, t):
         return pltpu.make_async_remote_copy(
@@ -92,10 +89,29 @@
             src_ref=buf.at[way, t], dst_ref=buf.at[2 + way, t], send_sem=pass_sem.at[way, t],
             recv_sem=recv_sem.at[2 + way, t], device_id={"blk": blk, "gshard": other}, device_id_type=MESH)
 
-    for t in range(min(2, steps)):
-        for way in range(2):
-            h = t if way == 0 else 1 - t
-            ring_copy(own.at[pl.ds(h * half, half)], way, t).start()
+    cuts = cut_send.shape[1]
+    width = rows // cuts
+
+    def cut(way, q):
+        return buf.at[way, last, :, pl.ds(q * width, width)]
+
+    def cut_copy(way, q):
+        return pltpu.make_async_remote_copy(
+            src_ref=buf.at[way, last - 2, :, pl.ds(q * width, width)], dst_ref=cut(way, q),
+            send_sem=cut_send.at[way, q], recv_sem=cut_recv.at[way, q],
+            device_id={"blk": right if way == 0 else left, "gshard": core}, device_id_type=MESH)
+
+    def cut_pass_copy(way, q):
+        return pltpu.make_async_remote_copy(
+            src_ref=cut(way, q), dst_ref=cut(2 + way, q), send_sem=cut_pass.at[way, q],
+            recv_sem=cut_recv.at[2 + way, q], device_id={"blk": blk, "gshard": other}, device_id_type=MESH)
+
+    def own_copy(way, t):
+        h = t if way == 0 else 1 - t
+        return ring_copy(own.at[pl.ds(h * half, half)], way, t)
+
+    for way in range(2):
+        own_copy(way, 0).start()
     sib_copy = pltpu.make_async_remote_copy(
         src_ref=own, dst_ref=sib_own, send_sem=sib_sem.at[0], recv_sem=sib_sem.at[1],
         device_id={"blk": blk, "gshard": other}, device_id_type=MESH)
@@ -126,6 +142,9 @@
         return carry
 
     lax.fori_loop(0, 2 * count, first, 0)
+    if steps > 1:
+        for way in range(2):
+            own_copy(way, 1).start()
     next_w(jnp.int32(1))
     w_copy(jnp.int32(1)).wait()
     sib_copy.wait_recv()
@@ -156,9 +175,14 @@
         for way in range(2):
             ring_copy(buf.at[way, t], way, t).wait_recv()
 
-            @pl.when(t + 2 < steps)
+            @pl.when(t + 2 < last)
             def _():
                 ring_copy(buf.at[way, t], way, t + 2).start()
+
+            @pl.when(t + 2 == last)
+            def _():
+                for q in range(cuts):
+                    cut_copy(way, q).start()
 
             pass_copy(way, t).start()
 
@@ -190,24 +214,32 @@
             scaled = (acc[h, f] * coup[f]).astype(jnp.bfloat16)
             parts[h, f] = jnp.dot(own[...], scaled, preferred_element_type=jnp.float32)
 
-    def met(side, f, h):
+    def met(side, f, h, q):
+        columns = pl.ds(q * width, width)
         return coup[f] * lax.dot_general(
-            far[side, f], buf[2 * side + h, last], (((1,), (1,)), ((), ())), preferred_element_type=jnp.float32)
-
-    for way in range(2):
-        ring_copy(buf.at[way, last], way, last).wait_recv()
-        pass_copy(way, last).start()
-    for h in range(2):
-        for f in range(count):
-            parts[h, f] += met(0, f, h)
+            far[side, f, :, columns], buf[2 * side + h, last, :, columns], (((1,), (1,)), ((), ())),
+            preferred_element_type=jnp.float32)
+
+    for q in range(cuts):
+        for way in range(2):
+            cut_copy(way, q).wait_recv()
+            cut_pass_copy(way, q).start()
+        for h in range(2):
+            for f in range(count):
+                parts[h, f] += met(0, f, h, q)
+        if q < cuts - 1:
+            for h in range(2):
+                cut_pass_copy(h, q).wait_recv()
+                for f in range(count):
+                    parts[h, f] += met(1, f, h, q)
 
     pair_rows = own.shape[0]
     row_k = lax.rem(lax.broadcasted_iota(jnp.int32, (pair_rows, half), 0), summed)
     same = row_k == lax.rem(lax.broadcasted_iota(jnp.int32, (pair_rows, half), 1), summed)
     for h in range(2):
-        pass_copy(h, last).wait_recv()
+        cut_pass_copy(h, cuts - 1).wait_recv()
         for f in range(count):
-            part = parts[h, f] + met(1, f, h)
+            part = parts[h, f] + met(1, f, h, cuts - 1)
             kept = jnp.where(same, part, 0.0).reshape(targets, summed, half).sum(axis=1)
             for n in range(targets):
                 red_send[n, pl.ds(f, 1), pl.ds(h * half, half)] = kept[n:n + 1, :]
@@ -230,7 +262,13 @@
             recv_sem=red_rsem.at[j], device_id=device(j), device_id_type=MESH).wait_recv()
         return so_far + red_recv[j]
 
-    out[...] = lax.fori_loop(1, devices, arrive, red_send[pl.ds(lax.div(me, group) * share, share)])
+    sums = lax.fori_loop(1, devices, arrive, red_send[pl.ds(lax.div(me, group) * share, share)])
+    pick = jnp.where(
+        lax.div(lax.broadcasted_iota(jnp.int32, (pair_rows, targets), 0), summed)
+        == lax.broadcasted_iota(jnp.int32, (pair_rows, targets), 1), 1.0, 0.0)
+    for n in range(share):
+        out[:, pl.ds(n * targets, targets)] = jnp.dot(
+            sums[n], pick, precision=lax.Precision.HIGHEST, preferred_element_type=jnp.float32)
 
     def sent(o, carry):
         red_copy(lax.rem(me + o, devices)).wait_send()
@@ -245,7 +283,11 @@
             pass_copy(way, t).wait_send()
         return carry
 
-    lax.fori_loop(0, steps, drained, 0)
+    lax.fori_loop(0, last, drained, 0)
+    for q in range(cuts):
+        for way in range(2):
+            cut_copy(way, q).wait_send()
+            cut_pass_copy(way, q).wait_send()
 
 
 def local(chips, screened, pairs, energies, nodes, qweights):
@@ -256,12 +298,13 @@
     steps = chips - 1
     devices = 2 * chips
     share = max(1, targets // devices)
+    cuts = max(1, rows // 256)
     smem = pl.BlockSpec(memory_space=pltpu.SMEM)
     vmem = pl.BlockSpec(memory_space=pltpu.VMEM)
     dma = pltpu.SemaphoreType.DMA
-    grouped = pl.pallas_call(
+    sigma = pl.pallas_call(
         functools.partial(kernel, chips, targets, summed),
-        out_shape=jax.ShapeDtypeStruct((share, count, pair_rows), jnp.float32),
+        out_shape=jax.ShapeDtypeStruct((count, share * targets), jnp.float32),
         in_specs=[pl.BlockSpec(memory_space=pl.ANY), vmem, smem, smem, smem],
         out_specs=vmem,
         scratch_shapes=[
@@ -275,6 +318,9 @@
             pltpu.VMEM((targets, count, pair_rows), jnp.float32),
             pltpu.VMEM((devices, share, count, pair_rows), jnp.float32),
             dma((SLOTS,)),
+            dma((2, cuts)),
+            dma((4, cuts)),
+            dma((2, cuts)),
             dma((2, steps)),
             dma((4, steps)),
             dma((2, steps)),
@@ -291,8 +337,6 @@
             transcendentals=0,
         ),
     )(screened, pairs.reshape(pair_rows, rows), energies, nodes, qweights)
-    sigma = grouped.reshape(share, count, targets, summed).sum(axis=3)
-    sigma = sigma.transpose(1, 0, 2).reshape(count, share * targets)
     width = targets * targets // devices
     if width < share * targets:
         me = lax.axis_index("blk") * 2 + lax.axis_index("gshard")

time: 98.9 us -> 98.3 us (level)
    reshape x2 -> x0, local copies, waits for them, and re-layouts: 1.43 us -> none  [the longest x1 0.78 us: local(): sigma = grouped.reshape(share, count, targets, summed).sum(axis=3)]
    unnamed x0 -> x1, local copies, waits for them, and re-layouts: none -> 1.24 us
where the time goes in v3:
time: 98.3 us; the launch traced here: 98.1 us
  Pallas kernels  96.9 us (99%)
  local copies, waits for them, and re-layouts  1.24 us (1%)
    pallas_call x1, Pallas kernels, local(): pl.pallas_call(functools.partial(kernel, chips, targets, summed), out_sha...  96.9 us

profile of v3, /device:TPU:0, one launch (start us, length us, event | category | flops | bytes accessed | tf_op | source)
XLA Modules:
  0.0 98.1 jit_solution(6012804505903314435)
XLA Ops:
  0.0 96.9 %shard_map.55 = f32[2,64]{1,0:T(2,128)} custom-call(bf16[2,1024,16384]{2,1,0:T(8,128)(2,1)} %w_hbm.1, bf16[512,1024]{1,0:T(8,128)(2,1)} %bitcast.1, f32[16]{0:T(128)} %energies.1, f32[2]{0:T(128)} %nodes.1, f32[2]{0:T(128)} %qweights.1), custom_call_target="tpu_custom_call" | custom-call | flops 34359738368 | bytes 134217728 | tf_op jit(solution)/shard_map/pallas_call | solution.py:305
  96.9 1.2 %copy.7 = f32[2,64]{1,0:T(2,128)} copy(f32[2,64]{1,0:T(2,128)} %shard_map.55) | data formatting | bytes 1024
